TPU v7x, 256 devices: a whole 4x4x8 slice. The times are simulated.
256 devices in a mesh: dp: 4 (over z_hi, core), context: 64 (over z_lo, x, y).
Axes of the slice: x: 4, y: 4, z: 8 (z_hi: 2, z_lo: 4; z = z_hi * 4 + z_lo), core: 2. Of those that a mesh axis runs over, the one named last changes fastest.
Arguments:
- grad_out: bfloat16 [4, 16384, 1024], P('dp', 'context'), may hold values from -6 to 6
- gate: bfloat16 [4, 16384, 1024], P('dp', 'context'), may hold values from -1.5 to 1.5
- key_in: bfloat16 [4, 16384, 1024], P('dp', 'context'), may hold values from -0.59765625 to 0.59765625
- value_in: bfloat16 [4, 16384, 1024], P('dp', 'context'), may hold values from -6 to 6
- filters: float32 [1024, 16384], P('context'), may hold values from -0.375 to 0.375
Outputs:
- grad_gate: bfloat16 [4, 16384, 1024], P('dp', 'context')
- grad_key: bfloat16 [4, 16384, 1024], P('dp', 'context')
- grad_value: bfloat16 [4, 16384, 1024], P('dp', 'context')
- grad_filter: float32 [1024, 16384], P(('context', 'dp'))
All inputs are finite; a program needn't handle non-finite values.
Results may differ from a plain program's by a relative error of at most 0.015.
Values may be sent and summed in bfloat16 or wider, within the bound.
A program may use at most 128 MiB of HBM per device.

v0:
```python
import functools

import jax
import jax.numpy as jnp
import numpy as np
from jax import lax
from jax.experimental import pallas as pl
from jax.experimental.pallas import tpu as pltpu
from jax.sharding import PartitionSpec as P

MESH = pl.DeviceIdType.MESH
F32 = jnp.float32
BF16 = jnp.bfloat16

SPAN = 256
PARTS = 64
OWN = 16
HALF = 8
LENGTH = SPAN * PARTS


def tables():
    k1 = np.arange(PARTS)[:, None] + 0.25
    p = np.arange(PARTS)[None, :]
    angle = 2 * np.pi * k1 * p / PARTS
    first = np.concatenate([np.cos(angle), -np.sin(angle)], 0)
    zero = np.zeros_like(first)
    pair = np.block([[first, zero], [zero, first]])
    filt = np.concatenate([first, first], 1)
    last = np.concatenate([np.cos(angle).T, -np.sin(angle).T], 1) / LENGTH
    s = np.arange(SPAN)
    twist = 2 * np.pi * k1 * s[None, :] / LENGTH
    grid = 2 * np.pi * (s[:, None] * s[None, :] % SPAN) / SPAN
    cos, sin = np.cos(grid), np.sin(grid)
    forward = np.block([[cos, -sin], [sin, cos]])
    inverse = np.block([[cos, sin], [-sin, cos]])
    place = np.zeros((2, SPAN, 2 * SPAN))
    for h in range(2):
        for j in range(SPAN // OWN):
            for a in range(2):
                for c in range(HALF):
                    place[h, j * OWN + a * HALF + c, a * SPAN + j * OWN + h * HALF + c] = 1
    narrow = [np.asarray(t, dtype=jnp.bfloat16) for t in (pair, filt, last, forward, inverse)]
    return (
        *narrow,
        np.cos(twist).astype(np.float32),
        np.sin(twist).astype(np.float32),
        np.asarray(place, dtype=jnp.bfloat16),
        np.asarray(np.eye(SPAN), dtype=jnp.bfloat16),
    )


def dot(a, b):
    return jnp.dot(a, b, preferred_element_type=F32)


def dot_t(a, b):
    return lax.dot_general(a, b, (((1,), (1,)), ((), ())), preferred_element_type=F32)


def target(me, k):
    z, x, y = me // 16, (me // 4) % 4, me % 4
    return ((z + k % 4) % 4) * 16 + ((x + (k // 4) % 4) % 4) * 4 + (y + k // 16) % 4


def kernel(
    go, gt, ki, vi, flt, pair, filt, last, fwd, inv, tcos, tsin, place, eye,
    out_gate, out_key, out_value, out_filter,
    send_a, recv_a, send_b, recv_b, wide, back_wide, spec, lag, lag_out, lag_in, far_out, far_in,
    ss_a, rs_a, ss_b, rs_b, ss_l, rs_l, ss_f, rs_f,
):
    dp, me = lax.axis_index("dp"), lax.axis_index("context")
    z_hi, core = dp // 2, dp % 2
    other_core = z_hi * 2 + (1 - core)
    other_cube = (1 - z_hi) * 2 + core

    barrier = pltpu.get_barrier_semaphore()

    def greet(k, carry):
        pl.semaphore_signal(
            barrier, inc=1, device_id={"context": target(me, k)}, device_id_type=MESH
        )
        return carry

    lax.fori_loop(1, PARTS, greet, 0)
    pl.semaphore_signal(barrier, inc=1, device_id={"dp": other_core}, device_id_type=MESH)
    pl.semaphore_signal(barrier, inc=1, device_id={"dp": other_cube}, device_id_type=MESH)

    for b in range(4):
        cols = pl.ds(b * SPAN, SPAN)
        kv = (ki[:, cols].astype(F32) * vi[:, cols].astype(F32)).astype(BF16)
        gg = (go[:, cols].astype(F32) * gt[:, cols].astype(F32)).astype(BF16)
        both = jnp.concatenate([kv, gg], axis=1)
        for h in range(2):
            rows = dot_t(place[h], both).astype(BF16)
            send_a[h, pl.ds(b * 16, 16)] = rows.reshape(16, OWN, SPAN)

    pl.semaphore_wait(barrier, PARTS + 1)

    def scatter(src, dst, ssem, rsem, h):
        def one(k, carry):
            d = target(me, k)
            pltpu.make_async_remote_copy(
                src_ref=src.at[h, d],
                dst_ref=dst.at[h, me],
                send_sem=ssem.at[h],
                recv_sem=rsem.at[h],
                device_id={"context": d},
                device_id_type=MESH,
            ).start()
            return carry

        lax.fori_loop(1, PARTS, one, 0)
        dst[h, me] = src[h, me]

    def whole(src, dst, ssem, rsem, h):
        return pltpu.make_async_remote_copy(
            src_ref=src.at[h, pl.ds(0, PARTS - 1)],
            dst_ref=dst.at[h, pl.ds(0, PARTS - 1)],
            send_sem=ssem.at[h],
            recv_sem=rsem.at[h],
            device_id={"context": me},
            device_id_type=MESH,
        )

    order = (1 - z_hi, z_hi)
    for h in order:
        scatter(send_a, recv_a, ss_a, rs_a, h)

    def lay(p, carry):
        cols = pl.ds(pl.multiple_of(p * SPAN, SPAN), SPAN)
        for lanes in range(2):
            wide[lanes, pl.ds(pl.multiple_of(p * OWN, OWN), OWN), :] = flt[
                :, pl.ds(pl.multiple_of(p * SPAN + lanes * 128, 128), 128)
            ]
        return carry

    lax.fori_loop(0, PARTS, lay, 0)

    def column(ref, row):
        return jnp.concatenate(
            [ref[lanes, pl.ds(row, PARTS, stride=OWN), :] for lanes in range(2)], axis=1
        )

    def twist(mid):
        re, im = mid[:PARTS], mid[PARTS:]
        c, s = tcos[...], tsin[...]
        return jnp.concatenate([re * c + im * s, im * c - re * s], axis=1).astype(BF16)

    def filter_pair(i, carry):
        mids = []
        for n in range(2):
            x = column(wide, 2 * i + n)
            high = x.astype(BF16)
            low = (x - high.astype(F32)).astype(BF16)
            mids.append(twist(dot(filt[...], jnp.concatenate([high, low], axis=0))))
        full = dot(jnp.concatenate(mids, axis=0), fwd[...])
        spec[pl.ds(2 * i, 2)] = full.reshape(2, PARTS, 2 * SPAN)
        return carry

    lax.fori_loop(0, OWN // 2, filter_pair, 0)

    def convolve(h, slot):
        for lanes in range(2):
            wide[lanes] = (
                recv_a[h, :, :, pl.ds(lanes * 128, 128)].astype(F32).reshape(PARTS * OWN, 128)
            )

        def channel_pair(i, carry):
            mids = []
            for n in range(2):
                c = 2 * i + n
                x = jnp.concatenate([column(wide, c), column(wide, HALF + c)], axis=0)
                mid = dot(pair[...], x.astype(BF16))
                mids += [twist(mid[: 2 * PARTS]), twist(mid[2 * PARTS :])]
            full = dot(jnp.concatenate(mids, axis=0), fwd[...])
            prods = []
            for n in range(2):
                f = spec[h * HALF + 2 * i + n]
                fr, fi = f[:, :SPAN], f[:, SPAN:]
                kv = full[2 * n * PARTS : (2 * n + 1) * PARTS]
                gg = full[(2 * n + 1) * PARTS : (2 * n + 2) * PARTS]
                kr, kj = kv[:, :SPAN], kv[:, SPAN:]
                gr, gj = gg[:, :SPAN], gg[:, SPAN:]
                prods += [
                    jnp.concatenate([fr * kr - fi * kj, fr * kj + fi * kr], axis=1),
                    jnp.concatenate([gr * fr + gj * fi, gj * fr - gr * fi], axis=1),
                    jnp.concatenate([gr * kr + gj * kj, gj * kr - gr * kj], axis=1),
                ]
            mid = dot(jnp.concatenate([q.astype(BF16) for q in prods], axis=0), inv[...])
            co, si = tcos[...], tsin[...]
            for n in range(2):
                c = 2 * i + n
                for a in range(3):
                    top = (3 * n + a) * PARTS
                    re, im = mid[top : top + PARTS, :SPAN], mid[top : top + PARTS, SPAN:]
                    y = jnp.concatenate([re * co - im * si, im * co + re * si], axis=0)
                    line = dot(last[...], y.astype(BF16))
                    for lanes in range(2):
                        piece = line[:, lanes * 128 : (lanes + 1) * 128]
                        if a < 2:
                            back_wide[lanes, pl.ds(a * HALF + c, PARTS, stride=OWN), :] = piece
                        else:
                            lag[slot, c // 4, lanes, pl.ds(c % 4, PARTS, stride=4), :] = piece
            return carry

        lax.fori_loop(0, HALF // 2, channel_pair, 0)
        for lanes in range(2):
            send_b[h, :, :, pl.ds(lanes * 128, 128)] = (
                back_wide[lanes].astype(BF16).reshape(PARTS, OWN, 128)
            )

    def lag_swap(slot):
        return pltpu.make_async_remote_copy(
            src_ref=lag_out.at[slot],
            dst_ref=lag_in.at[slot],
            send_sem=ss_l.at[slot],
            recv_sem=rs_l.at[slot],
            device_id={"dp": other_core},
            device_id_type=MESH,
        )

    far = pltpu.make_async_remote_copy(
        src_ref=far_out,
        dst_ref=far_in,
        send_sem=ss_f.at[0],
        recv_sem=rs_f.at[0],
        device_id={"dp": other_cube},
        device_id_type=MESH,
    )

    for slot, h in enumerate(order):
        whole(send_a, recv_a, ss_a, rs_a, h).wait_recv()
        if slot == 1:
            lag_swap(0).wait_recv()
            far_out[...] = (lag[0, core] + lag_in[0].astype(F32)).astype(BF16)
            far.start()
        convolve(h, slot)
        scatter(send_b, recv_b, ss_b, rs_b, h)
        lag_out[slot] = lag[slot, 1 - core].astype(BF16)
        lag_swap(slot).start()

    lag_swap(1).wait_recv()
    far.wait_recv()
    for lanes in range(2):
        total = lag[1, core, lanes] + lag_in[1, lanes].astype(F32) + far_in[lanes].astype(F32)
        for p in range(PARTS):
            out_filter[:, pl.ds(p * SPAN + lanes * 128, 128)] = total[4 * p : 4 * p + 4]

    for h in order:
        whole(send_b, recv_b, ss_b, rs_b, h).wait_recv()
    for b in range(4):
        cols = pl.ds(b * SPAN, SPAN)
        groups = [recv_b[h, pl.ds(b * 16, 16)].astype(F32) for h in range(2)]
        turned = []
        for a in range(2):
            rows = jnp.concatenate([g[:, a * HALF : (a + 1) * HALF] for g in groups], axis=1)
            turned.append(dot_t(eye[...], rows.reshape(SPAN, SPAN).astype(BF16)))
        conv, back = turned
        out_gate[:, cols] = (go[:, cols].astype(F32) * conv).astype(BF16)
        out_key[:, cols] = (back * vi[:, cols].astype(F32)).astype(BF16)
        out_value[:, cols] = (back * ki[:, cols].astype(F32)).astype(BF16)

    for h in order:
        whole(send_a, recv_a, ss_a, rs_a, h).wait_send()
        whole(send_b, recv_b, ss_b, rs_b, h).wait_send()
    for slot in range(2):
        lag_swap(slot).wait_send()
    far.wait_send()


def on_device(grad_out, gate, key_in, value_in, filters):
    vmem = pl.BlockSpec(memory_space=pltpu.VMEM)
    consts = [jnp.asarray(t) for t in tables()]
    blocks = (2, PARTS, OWN, SPAN)
    dma = pltpu.SemaphoreType.DMA
    seq = jax.ShapeDtypeStruct((SPAN, 1024), BF16)
    grads = pl.pallas_call(
        kernel,
        out_shape=(seq, seq, seq, jax.ShapeDtypeStruct((4, LENGTH), F32)),
        in_specs=[vmem] * (5 + len(consts)),
        out_specs=(vmem,) * 4,
        scratch_shapes=[
            pltpu.VMEM(blocks, BF16),
            pltpu.VMEM(blocks, BF16),
            pltpu.VMEM(blocks, BF16),
            pltpu.VMEM(blocks, BF16),
            pltpu.VMEM((2, PARTS * OWN, 128), F32),
            pltpu.VMEM((2, PARTS * OWN, 128), F32),
            pltpu.VMEM((OWN, PARTS, 2 * SPAN), F32),
            pltpu.VMEM((2, 2, 2, PARTS * 4, 128), F32),
            pltpu.VMEM((2, 2, PARTS * 4, 128), BF16),
            pltpu.VMEM((2, 2, PARTS * 4, 128), BF16),
            pltpu.VMEM((2, PARTS * 4, 128), BF16),
            pltpu.VMEM((2, PARTS * 4, 128), BF16),
            dma((2,)), dma((2,)), dma((2,)), dma((2,)),
            dma((2,)), dma((2,)), dma((1,)), dma((1,)),
        ],
        name="hyena_backward",
        compiler_params=pltpu.CompilerParams(
            collective_id=0, has_side_effects=True, vmem_limit_bytes=48 * 2**20
        ),
    )(grad_out[0], gate[0], key_in[0], value_in[0], filters, *consts)
    return (grads[0][None], grads[1][None], grads[2][None], grads[3])


def solution(mesh):
    return jax.shard_map(
        on_device,
        mesh=mesh,
        in_specs=(
            P("dp", "context", None),
            P("dp", "context", None),
            P("dp", "context", None),
            P("dp", "context", None),
            P("context", None),
        ),
        out_specs=(
            P("dp", "context", None),
            P("dp", "context", None),
            P("dp", "context", None),
            P(("context", "dp"), None),
        ),
        check_vma=False,
    )
```

profile of v0, /device:TPU:1, one launch (start us, length us, event | category | flops | bytes accessed | tf_op | source)
XLA Modules:
  0.0 82.6 jit_solution(7044419231040828780)
XLA Ops:
  0.6 0.0 copy-start
  0.6 1.0 %copy-done = bf16[1,256,1024]{2,1,0:T(8,128)(2,1)S(1)} copy-done((bf16[1,256,1024]{2,1,0:T(8,128)(2,1)S(1)}, bf16[1,256,1024]{2,1,0:T(8,128)(2,1)}, u32[]{:S(2)}) %copy-start) | copy-done | bytes 524312
  1.7 0.0 copy-start.1
  1.7 1.0 %copy-done.1 = bf16[1,256,1024]{2,1,0:T(8,128)(2,1)S(1)} copy-done((bf16[1,256,1024]{2,1,0:T(8,128)(2,1)S(1)}, bf16[1,256,1024]{2,1,0:T(8,128)(2,1)}, u32[]{:S(2)}) %copy-start.1) | copy-done | bytes 524312
  2.7 0.0 copy-start.2
  2.7 1.0 %copy-done.2 = bf16[1,256,1024]{2,1,0:T(8,128)(2,1)S(1)} copy-done((bf16[1,256,1024]{2,1,0:T(8,128)(2,1)S(1)}, bf16[1,256,1024]{2,1,0:T(8,128)(2,1)}, u32[]{:S(2)}) %copy-start.2) | copy-done | bytes 524312
  3.8 0.0 copy-start.3
  3.8 1.0 %copy-done.3 = bf16[1,256,1024]{2,1,0:T(8,128)(2,1)S(1)} copy-done((bf16[1,256,1024]{2,1,0:T(8,128)(2,1)S(1)}, bf16[1,256,1024]{2,1,0:T(8,128)(2,1)}, u32[]{:S(2)}) %copy-start.3) | copy-done | bytes 524312
  4.8 0.0 copy-start.4
  4.8 1.0 %copy-done.4 = bf16[2,256,512]{2,1,0:T(8,128)(2,1)S(1)} copy-done((bf16[2,256,512]{2,1,0:T(8,128)(2,1)S(1)}, bf16[2,256,512]{2,1,0:T(8,128)(2,1)}, u32[]{:S(2)}) %copy-start.4) | copy-done | bytes 524312
  5.8 0.0 copy-start.5
  5.8 1.0 %copy-done.5 = bf16[512,512]{1,0:T(8,128)(2,1)S(1)} copy-done((bf16[512,512]{1,0:T(8,128)(2,1)S(1)}, bf16[512,512]{1,0:T(8,128)(2,1)}, u32[]{:S(2)}) %copy-start.5) | copy-done | bytes 524312
  6.9 0.0 copy-start.6
  6.9 1.0 %copy-done.6 = bf16[512,512]{1,0:T(8,128)(2,1)S(1)} copy-done((bf16[512,512]{1,0:T(8,128)(2,1)S(1)}, bf16[512,512]{1,0:T(8,128)(2,1)}, u32[]{:S(2)}) %copy-start.6) | copy-done | bytes 524312
  7.9 0.0 copy-start.7
  7.9 0.9 %copy-done.7 = bf16[256,256]{1,0:T(8,128)(2,1)S(1)} copy-done((bf16[256,256]{1,0:T(8,128)(2,1)S(1)}, bf16[256,256]{1,0:T(8,128)(2,1)}, u32[]{:S(2)}) %copy-start.7) | copy-done | bytes 131096
  8.8 0.0 copy-start.8
  8.8 0.8 %copy-done.8 = f32[64,256]{1,0:T(8,128)S(1)} copy-done((f32[64,256]{1,0:T(8,128)S(1)}, f32[64,256]{1,0:T(8,128)}, u32[]{:S(2)}) %copy-start.8) | copy-done | bytes 65560
  9.7 0.0 copy-start.9
  9.7 0.8 %copy-done.9 = f32[64,256]{1,0:T(8,128)S(1)} copy-done((f32[64,256]{1,0:T(8,128)S(1)}, f32[64,256]{1,0:T(8,128)}, u32[]{:S(2)}) %copy-start.9) | copy-done | bytes 65560
  10.5 0.0 copy-start.10
  10.5 0.8 %copy-done.10 = bf16[256,128]{1,0:T(8,128)(2,1)S(1)} copy-done((bf16[256,128]{1,0:T(8,128)(2,1)S(1)}, bf16[256,128]{1,0:T(8,128)(2,1)}, u32[]{:S(2)}) %copy-start.10) | copy-done | bytes 65560
  11.4 0.0 copy-start.11
  11.4 0.8 copy-done.11
  12.1 0.0 copy-start.12
  12.1 0.7 copy-done.12
  12.8 66.6 %hyena_backward.1 = (bf16[256,1024]{1,0:T(8,128)(2,1)S(1)}, bf16[256,1024]{1,0:T(8,128)(2,1)S(1)}, bf16[256,1024]{1,0:T(8,128)(2,1)S(1)}, f32[4,16384]{1,0:T(4,128)S(1)}) custom-call(bf16[256,1024]{1,0:T(8,128)(2,1)S(1)} %bitcast.7, bf16[256,1024]{1,0:T(8,128)(2,1)S(1)} %bitcast.8, bf16[256,1024]{1,0:T(8,128)(2,1)S(1)} %bitcast.9, ...), custom_call_target="tpu_custom_call" | custom-call | tf_op jit(solution)/shard_map/hyena_backward/pallas_call | solution.py:278
  79.5 0.8 copy.22
  80.3 0.8 copy.23
  81.1 0.8 copy.24
  81.9 0.7 copy.25
Async XLA Ops:
  0.6 1.0 %copy-start = (bf16[1,256,1024]{2,1,0:T(8,128)(2,1)S(1)}, bf16[1,256,1024]{2,1,0:T(8,128)(2,1)}, u32[]{:S(2)}) copy-start(bf16[1,256,1024]{2,1,0:T(8,128)(2,1)} %param.14) | copy-start | bytes 1572868
  1.7 1.0 %copy-start.1 = (bf16[1,256,1024]{2,1,0:T(8,128)(2,1)S(1)}, bf16[1,256,1024]{2,1,0:T(8,128)(2,1)}, u32[]{:S(2)}) copy-start(bf16[1,256,1024]{2,1,0:T(8,128)(2,1)} %param.15) | copy-start | bytes 1572868
  2.7 1.0 %copy-start.2 = (bf16[1,256,1024]{2,1,0:T(8,128)(2,1)S(1)}, bf16[1,256,1024]{2,1,0:T(8,128)(2,1)}, u32[]{:S(2)}) copy-start(bf16[1,256,1024]{2,1,0:T(8,128)(2,1)} %param.16) | copy-start | bytes 1572868
  3.8 1.0 %copy-start.3 = (bf16[1,256,1024]{2,1,0:T(8,128)(2,1)S(1)}, bf16[1,256,1024]{2,1,0:T(8,128)(2,1)}, u32[]{:S(2)}) copy-start(bf16[1,256,1024]{2,1,0:T(8,128)(2,1)} %param.17) | copy-start | bytes 1572868
  4.8 1.0 %copy-start.4 = (bf16[2,256,512]{2,1,0:T(8,128)(2,1)S(1)}, bf16[2,256,512]{2,1,0:T(8,128)(2,1)}, u32[]{:S(2)}) copy-start(bf16[2,256,512]{2,1,0:T(8,128)(2,1)} %constant.25.clone.place) | copy-start | bytes 1572868
  5.8 1.0 %copy-start.5 = (bf16[512,512]{1,0:T(8,128)(2,1)S(1)}, bf16[512,512]{1,0:T(8,128)(2,1)}, u32[]{:S(2)}) copy-start(bf16[512,512]{1,0:T(8,128)(2,1)} %constant.22.clone.inv) | copy-start | bytes 1572868
  6.9 1.0 %copy-start.6 = (bf16[512,512]{1,0:T(8,128)(2,1)S(1)}, bf16[512,512]{1,0:T(8,128)(2,1)}, u32[]{:S(2)}) copy-start(bf16[512,512]{1,0:T(8,128)(2,1)} %constant.21.clone.fwd) | copy-start | bytes 1572868
  7.9 0.9 %copy-start.7 = (bf16[256,256]{1,0:T(8,128)(2,1)S(1)}, bf16[256,256]{1,0:T(8,128)(2,1)}, u32[]{:S(2)}) copy-start(bf16[256,256]{1,0:T(8,128)(2,1)} %constant.26.clone.eye) | copy-start | bytes 393220
  8.8 0.8 %copy-start.8 = (f32[64,256]{1,0:T(8,128)S(1)}, f32[64,256]{1,0:T(8,128)}, u32[]{:S(2)}) copy-start(f32[64,256]{1,0:T(8,128)} %constant.24.clone.tsin) | copy-start | bytes 196612
  9.7 0.8 %copy-start.9 = (f32[64,256]{1,0:T(8,128)S(1)}, f32[64,256]{1,0:T(8,128)}, u32[]{:S(2)}) copy-start(f32[64,256]{1,0:T(8,128)} %constant.23.clone.tcos) | copy-start | bytes 196612
  10.5 0.8 %copy-start.10 = (bf16[256,128]{1,0:T(8,128)(2,1)S(1)}, bf16[256,128]{1,0:T(8,128)(2,1)}, u32[]{:S(2)}) copy-start(bf16[256,128]{1,0:T(8,128)(2,1)} %constant.18.clone.pair) | copy-start | bytes 196612
  11.4 0.8 copy-start.11
  12.1 0.7 copy-start.12
where the time goes:
time: 83.3 us; the launch traced here: 82.6 us
  Pallas kernels  66.6 us (80%)
  local copies, waits for them, and re-layouts  15.3 us (18%)
    pallas_call x1, Pallas kernels, on_device(): pl.pallas_call(kernel, out_shape=(seq, seq, seq, jax.ShapeDtypeStruct((4,...  66.6 us
    unnamed x30, local copies, waits for them, and re-layouts  15.3 us

commit v1 on v0

--- a/solution.py
+++ b/solution.py
@@ -17,6 +17,7 @@
 OWN = 16
 HALF = 8
 LENGTH = SPAN * PARTS
+OPERANDS = 14
 
 
 def tables():
@@ -40,14 +41,8 @@
             for a in range(2):
                 for c in range(HALF):
                     place[h, j * OWN + a * HALF + c, a * SPAN + j * OWN + h * HALF + c] = 1
-    narrow = [np.asarray(t, dtype=jnp.bfloat16) for t in (pair, filt, last, forward, inverse)]
-    return (
-        *narrow,
-        np.cos(twist).astype(np.float32),
-        np.sin(twist).astype(np.float32),
-        np.asarray(place, dtype=jnp.bfloat16),
-        np.asarray(np.eye(SPAN), dtype=jnp.bfloat16),
-    )
+    eye = np.eye(SPAN)
+    return place, filt, np.cos(twist), np.sin(twist), forward, pair, inverse, last, eye
 
 
 def dot(a, b):
@@ -58,15 +53,29 @@
     return lax.dot_general(a, b, (((1,), (1,)), ((), ())), preferred_element_type=F32)
 
 
-def target(me, k):
-    z, x, y = me // 16, (me // 4) % 4, me % 4
-    return ((z + k % 4) % 4) * 16 + ((x + (k // 4) % 4) % 4) * 4 + (y + k // 16) % 4
-
-
-def kernel(
-    go, gt, ki, vi, flt, pair, filt, last, fwd, inv, tcos, tsin, place, eye,
-    out_gate, out_key, out_value, out_filter,
-    send_a, recv_a, send_b, recv_b, wide, back_wide, spec, lag, lag_out, lag_in, far_out, far_in,
+def target(me, plane, k):
+    x, y = (me // 4) % 4, me % 4
+    return plane * 16 + ((x + k // 4) % 4) * 4 + (y + k % 4) % 4
+
+
+def kernel(*refs):
+    given, refs = refs[:OPERANDS], refs[OPERANDS:]
+    results, refs = refs[:3], refs[3:]
+    held, loaded, refs = refs[:OPERANDS], refs[OPERANDS], refs[OPERANDS + 1 :]
+    loads = [
+        pltpu.make_async_copy(src, dst, loaded.at[n])
+        for n, (src, dst) in enumerate(zip(given, held))
+    ]
+    for load in loads:
+        load.start()
+    body(loads, *held, *results, *refs)
+
+
+def body(
+    loads,
+    gt, ki, vi, go, place, flt, filt, tcos, tsin, fwd, pair, inv, last, eye,
+    out_conv, out_back, out_filter,
+    both, send_a, recv_a, send_b, recv_b, wide, back_wide, spec, lag, lag_out, lag_in, far_out, far_in,
     ss_a, rs_a, ss_b, rs_b, ss_l, rs_l, ss_f, rs_f,
 ):
     dp, me = lax.axis_index("dp"), lax.axis_index("context")
@@ -76,42 +85,76 @@
 
     barrier = pltpu.get_barrier_semaphore()
 
-    def greet(k, carry):
-        pl.semaphore_signal(
-            barrier, inc=1, device_id={"context": target(me, k)}, device_id_type=MESH
-        )
-        return carry
-
-    lax.fori_loop(1, PARTS, greet, 0)
+    z = me // 16
+    half, odd = z // 2, z % 2
+    across, behind = (1 - half) * 2 + odd, (1 - half) * 2 + (1 - odd)
+    beside = half * 2 + (1 - odd)
+    planes = (across, behind, beside, z)
+
+    for plane in planes:
+
+        def greet(k, carry, plane=plane):
+            pl.semaphore_signal(
+                barrier, inc=1, device_id={"context": target(me, plane, k)}, device_id_type=MESH
+            )
+            return carry
+
+        lax.fori_loop(1 if plane is z else 0, 16, greet, 0)
     pl.semaphore_signal(barrier, inc=1, device_id={"dp": other_core}, device_id_type=MESH)
     pl.semaphore_signal(barrier, inc=1, device_id={"dp": other_cube}, device_id_type=MESH)
 
-    for b in range(4):
-        cols = pl.ds(b * SPAN, SPAN)
+    for load in loads[:5]:
+        load.wait()
+    order = (1 - z_hi, z_hi)
+
+    def rows_of(h, plane):
+        rows = dot_t(place[h], both[plane]).astype(BF16)
+        send_a[h, pl.ds(plane * 16, 16)] = rows.reshape(16, OWN, SPAN)
+
+    def send(src, dst, ssem, rsem, h, plane, k):
+        d = target(me, plane, k)
+        pltpu.make_async_remote_copy(
+            src_ref=src.at[h, d],
+            dst_ref=dst.at[h, me],
+            send_sem=ssem.at[h],
+            recv_sem=rsem.at[h],
+            device_id={"context": d},
+            device_id_type=MESH,
+        ).start()
+
+    def send_planes(src, dst, ssem, rsem, jobs):
+        def one(k, carry):
+            for h, plane in jobs:
+                send(src, dst, ssem, rsem, h, plane, k)
+            return carry
+
+        lax.fori_loop(1, 16, one, 0)
+        for h, plane in jobs:
+            if plane is z:
+                dst[h, me] = src[h, me]
+            else:
+                send(src, dst, ssem, rsem, h, plane, 0)
+
+    first, second = order
+    for n, plane in enumerate(planes):
+        cols = pl.ds(pl.multiple_of(plane * SPAN, SPAN), SPAN)
         kv = (ki[:, cols].astype(F32) * vi[:, cols].astype(F32)).astype(BF16)
         gg = (go[:, cols].astype(F32) * gt[:, cols].astype(F32)).astype(BF16)
-        both = jnp.concatenate([kv, gg], axis=1)
-        for h in range(2):
-            rows = dot_t(place[h], both).astype(BF16)
-            send_a[h, pl.ds(b * 16, 16)] = rows.reshape(16, OWN, SPAN)
-
-    pl.semaphore_wait(barrier, PARTS + 1)
-
-    def scatter(src, dst, ssem, rsem, h):
-        def one(k, carry):
-            d = target(me, k)
-            pltpu.make_async_remote_copy(
-                src_ref=src.at[h, d],
-                dst_ref=dst.at[h, me],
-                send_sem=ssem.at[h],
-                recv_sem=rsem.at[h],
-                device_id={"context": d},
-                device_id_type=MESH,
-            ).start()
-            return carry
-
-        lax.fori_loop(1, PARTS, one, 0)
-        dst[h, me] = src[h, me]
+        both[plane] = jnp.concatenate([kv, gg], axis=1)
+        rows_of(first, plane)
+        if n == 0:
+            pl.semaphore_wait(barrier, PARTS + 1)
+        if n < 2:
+            send_planes(send_a, recv_a, ss_a, rs_a, [(first, plane)])
+    rows_of(second, across)
+    rows_of(second, behind)
+    send_planes(
+        send_a, recv_a, ss_a, rs_a,
+        [(first, beside), (second, across), (first, z), (second, behind)],
+    )
+    rows_of(second, beside)
+    rows_of(second, z)
+    send_planes(send_a, recv_a, ss_a, rs_a, [(second, beside), (second, z)])
 
     def whole(src, dst, ssem, rsem, h):
         return pltpu.make_async_remote_copy(
@@ -123,9 +166,8 @@
             device_id_type=MESH,
         )
 
-    order = (1 - z_hi, z_hi)
-    for h in order:
-        scatter(send_a, recv_a, ss_a, rs_a, h)
+    for load in loads[5:]:
+        load.wait()
 
     def lay(p, carry):
         cols = pl.ds(pl.multiple_of(p * SPAN, SPAN), SPAN)
@@ -236,7 +278,8 @@
             far_out[...] = (lag[0, core] + lag_in[0].astype(F32)).astype(BF16)
             far.start()
         convolve(h, slot)
-        scatter(send_b, recv_b, ss_b, rs_b, h)
+        send_planes(send_b, recv_b, ss_b, rs_b, [(h, across), (h, behind)])
+        send_planes(send_b, recv_b, ss_b, rs_b, [(h, beside), (h, z)])
         lag_out[slot] = lag[slot, 1 - core].astype(BF16)
         lag_swap(slot).start()
 
@@ -256,10 +299,8 @@
         for a in range(2):
             rows = jnp.concatenate([g[:, a * HALF : (a + 1) * HALF] for g in groups], axis=1)
             turned.append(dot_t(eye[...], rows.reshape(SPAN, SPAN).astype(BF16)))
-        conv, back = turned
-        out_gate[:, cols] = (go[:, cols].astype(F32) * conv).astype(BF16)
-        out_key[:, cols] = (back * vi[:, cols].astype(F32)).astype(BF16)
-        out_value[:, cols] = (back * ki[:, cols].astype(F32)).astype(BF16)
+        out_conv[:, cols] = turned[0].astype(BF16)
+        out_back[:, cols] = turned[1].astype(BF16)
 
     for h in order:
         whole(send_a, recv_a, ss_a, rs_a, h).wait_send()
@@ -271,16 +312,24 @@
 
 def on_device(grad_out, gate, key_in, value_in, filters):
     vmem = pl.BlockSpec(memory_space=pltpu.VMEM)
-    consts = [jnp.asarray(t) for t in tables()]
+    consts = [
+        jnp.asarray(t.astype(np.float32) if n in (2, 3) else np.asarray(t, dtype=jnp.bfloat16))
+        for n, t in enumerate(tables())
+    ]
+    place, *rest = consts
+    operands = (gate[0], key_in[0], value_in[0], grad_out[0], place, filters, *rest)
     blocks = (2, PARTS, OWN, SPAN)
     dma = pltpu.SemaphoreType.DMA
     seq = jax.ShapeDtypeStruct((SPAN, 1024), BF16)
-    grads = pl.pallas_call(
+    conv, back, grad_filter = pl.pallas_call(
         kernel,
-        out_shape=(seq, seq, seq, jax.ShapeDtypeStruct((4, LENGTH), F32)),
-        in_specs=[vmem] * (5 + len(consts)),
-        out_specs=(vmem,) * 4,
+        out_shape=(seq, seq, jax.ShapeDtypeStruct((4, LENGTH), F32)),
+        in_specs=[pl.BlockSpec(memory_space=pltpu.HBM)] * OPERANDS,
+        out_specs=(vmem,) * 3,
         scratch_shapes=[
+            *[pltpu.VMEM(x.shape, x.dtype) for x in operands],
+            dma((OPERANDS,)),
+            pltpu.VMEM((4, SPAN, 2 * SPAN), BF16),
             pltpu.VMEM(blocks, BF16),
             pltpu.VMEM(blocks, BF16),
             pltpu.VMEM(blocks, BF16),
@@ -298,10 +347,14 @@
         ],
         name="hyena_backward",
         compiler_params=pltpu.CompilerParams(
-            collective_id=0, has_side_effects=True, vmem_limit_bytes=48 * 2**20
+            collective_id=0, has_side_effects=True, vmem_limit_bytes=63 * 2**20
         ),
-    )(grad_out[0], gate[0], key_in[0], value_in[0], filters, *consts)
-    return (grads[0][None], grads[1][None], grads[2][None], grads[3])
+    )(*operands)
+    wide = back.astype(F32)
+    grad_gate = (grad_out[0].astype(F32) * conv.astype(F32)).astype(BF16)
+    grad_key = (wide * value_in[0].astype(F32)).astype(BF16)
+    grad_value = (wide * key_in[0].astype(F32)).astype(BF16)
+    return (grad_gate[None], grad_key[None], grad_value[None], grad_filter)
 
 
 def solution(mesh):

time: 83.3 us -> 71.1 us (0.85)
  local copies, waits for them, and re-layouts: 15.3 us -> 0.71 us
  other arithmetic: 0 us -> 3.11 us
    unnamed x30 -> x5, local copies, waits for them, and re-layouts: 15.3 us -> 0.71 us
    broadcast_in_dim x0 -> x1, other arithmetic: none -> 3.11 us  [on_device(): return (grad_gate[None], grad_key[None], grad_value[None], grad_filter)]
where the time goes in v1:
time: 71.1 us; the launch traced here: 71 us
  Pallas kernels  66.5 us (94%)
  other arithmetic  3.11 us (4%)
    pallas_call x1, Pallas kernels, on_device(): pl.pallas_call(kernel, out_shape=(seq, seq, jax.ShapeDtypeStruct((4, LENG...  66.5 us
    broadcast_in_dim x1, other arithmetic, on_device(): return (grad_gate[None], grad_key[None], grad_value[None], grad_filter)  3.11 us

profile of v1, /device:TPU:1, one launch (start us, length us, event | category | flops | bytes accessed | tf_op | source)
XLA Modules:
  0.0 71.0 jit_solution(3544320884115642031)
XLA Ops:
  0.6 0.0 copy-start
  0.6 66.5 %hyena_backward.1 = (bf16[256,1024]{1,0:T(8,128)(2,1)}, bf16[256,1024]{1,0:T(8,128)(2,1)}, f32[4,16384]{1,0:T(4,128)}) custom-call(bf16[256,1024]{1,0:T(8,128)(2,1)} %bitcast.16, bf16[256,1024]{1,0:T(8,128)(2,1)} %bitcast.13, bf16[256,1024]{1,0:T(8,128)(2,1)} %bitcast.14, bf16[256,1024]{1,0:T(8,128)(2,1)} %bitcast.15, ...), custom_call_target="tpu_custom_call" | custom-call | tf_op jit(solution)/shard_map/hyena_backward/pallas_call | solution.py:324
  67.2 0.0 copy-done
  67.2 0.0 copy-start.1
  67.2 3.1 %fusion.3 = (bf16[1,256,1024]{2,1,0:T(8,128)(2,1)}, bf16[1,256,1024]{2,1,0:T(8,128)(2,1)}, bf16[1,256,1024]{2,1,0:T(8,128)(2,1)}) fusion(bf16[256,1024]{1,0:T(8,128)(2,1)} %get-tuple-element.8, bf16[1,256,1024]{2,1,0:T(8,128)(2,1)S(1)} %copy-done, bf16[1,256,1024]{2,1,0:T(8,128)(2,1)} %param.17, bf16[256,1024]{1,0:T(8,128)(2,1)} %get-tuple-element.7, ...), kind=kLoop, calls=%fused_computation.6 | loop fusion | flops 2883584 | bytes 4194304 | tf_op jit(solution)/shard_map/broadcast_in_dim | solution.py:357
  70.3 0.0 copy-done.1
  70.3 0.7 copy.19
Async XLA Ops:
  0.6 66.5 %copy-start = (bf16[1,256,1024]{2,1,0:T(8,128)(2,1)S(1)}, bf16[1,256,1024]{2,1,0:T(8,128)(2,1)}, u32[]{:S(2)}) copy-start(bf16[1,256,1024]{2,1,0:T(8,128)(2,1)} %param.16) | copy-start | bytes 1572868
  67.2 3.1 %copy-start.1 = (f32[4,16384]{1,0:T(4,128)S(1)}, f32[4,16384]{1,0:T(4,128)}, u32[]{:S(2)}) copy-start(f32[4,16384]{1,0:T(4,128)} %get-tuple-element.20) | copy-start | bytes 786436

commit v2 on v1

--- a/solution.py
+++ b/solution.py
@@ -17,7 +17,8 @@
 OWN = 16
 HALF = 8
 LENGTH = SPAN * PARTS
-OPERANDS = 14
+SIDE = PARTS // 2
+OPERANDS = 18
 
 
 def tables():
@@ -42,7 +43,17 @@
                 for c in range(HALF):
                     place[h, j * OWN + a * HALF + c, a * SPAN + j * OWN + h * HALF + c] = 1
     eye = np.eye(SPAN)
-    return place, filt, np.cos(twist), np.sin(twist), forward, pair, inverse, last, eye
+    k1 = np.arange(SIDE)[:, None] + 0.25
+    angle = 2 * np.pi * k1 * np.arange(SIDE)[None, :] / SIDE
+    first = np.concatenate([np.cos(angle), -np.sin(angle)], 0)
+    near = np.block([[first, np.zeros_like(first)], [np.zeros_like(first), first]])
+    final = np.concatenate([np.cos(angle).T, -np.sin(angle).T], 1) * 2 / LENGTH
+    near_last = np.block([[final, np.zeros_like(final)], [np.zeros_like(final), final]])
+    near_twist = 2 * np.pi * k1 * s[None, :] * 2 / LENGTH
+    return (
+        np.cos(twist), np.sin(twist), np.cos(near_twist), np.sin(near_twist),
+        place, eye, filt, forward, near, pair, inverse, last, near_last,
+    )
 
 
 def dot(a, b):
@@ -73,10 +84,12 @@
 
 def body(
     loads,
-    gt, ki, vi, go, place, flt, filt, tcos, tsin, fwd, pair, inv, last, eye,
+    gt, ki, vi, go, place, eye, flt, tcos, tsin, near_cos, near_sin,
+    filt, fwd, near, pair, inv, last, near_last,
     out_conv, out_back, out_filter,
-    both, send_a, recv_a, send_b, recv_b, wide, back_wide, spec, lag, lag_out, lag_in, far_out, far_in,
-    ss_a, rs_a, ss_b, rs_b, ss_l, rs_l, ss_f, rs_f,
+    both, send_a, recv_a, send_b, recv_b, send_c, recv_c, work_a, work_in, work_b, work_back,
+    taps, near_taps, wide, back_wide, spec, near_spec, lag, lag_out, lag_in, far_out, far_in,
+    ss_a, rs_a, ss_b, rs_b, ss_c, rs_c, ss_w, rs_w, ss_t, rs_t, ss_l, rs_l, ss_f, rs_f,
 ):
     dp, me = lax.axis_index("dp"), lax.axis_index("context")
     z_hi, core = dp // 2, dp % 2
@@ -102,8 +115,10 @@
         lax.fori_loop(1 if plane is z else 0, 16, greet, 0)
     pl.semaphore_signal(barrier, inc=1, device_id={"dp": other_core}, device_id_type=MESH)
     pl.semaphore_signal(barrier, inc=1, device_id={"dp": other_cube}, device_id_type=MESH)
-
-    for load in loads[:5]:
+    twin = {"dp": other_cube, "context": (me + SIDE) % PARTS}
+    pl.semaphore_signal(barrier, inc=1, device_id=twin, device_id_type=MESH)
+
+    for load in loads[:7]:
         load.wait()
     order = (1 - z_hi, z_hi)
 
@@ -111,29 +126,59 @@
         rows = dot_t(place[h], both[plane]).astype(BF16)
         send_a[h, pl.ds(plane * 16, 16)] = rows.reshape(16, OWN, SPAN)
 
-    def send(src, dst, ssem, rsem, h, plane, k):
+    mine = me % SIDE
+
+    def forward_block(h):
+        return lambda d: (send_a.at[h, d], recv_a.at[h, me], ss_a.at[h], rs_a.at[h])
+
+    def work_block(d):
+        return work_a.at[d % SIDE], work_in.at[mine], ss_w.at[0], rs_w.at[0]
+
+    def return_block(h):
+        return lambda d: (send_b.at[h, d % SIDE], recv_b.at[h, mine], ss_b.at[h], rs_b.at[h])
+
+    def far_block(h):
+        return lambda d: (send_c.at[h, d % SIDE], recv_c.at[h, mine], ss_c.at[h], rs_c.at[h])
+
+    def work_result(d):
+        return work_b.at[d % SIDE], work_back.at[mine], ss_w.at[1], rs_w.at[1]
+
+    def send(block, plane, k):
         d = target(me, plane, k)
+        src, dst, ssem, rsem = block(d)
         pltpu.make_async_remote_copy(
-            src_ref=src.at[h, d],
-            dst_ref=dst.at[h, me],
-            send_sem=ssem.at[h],
-            recv_sem=rsem.at[h],
+            src_ref=src,
+            dst_ref=dst,
+            send_sem=ssem,
+            recv_sem=rsem,
             device_id={"context": d},
             device_id_type=MESH,
         ).start()
 
-    def send_planes(src, dst, ssem, rsem, jobs):
+    def send_planes(jobs):
         def one(k, carry):
-            for h, plane in jobs:
-                send(src, dst, ssem, rsem, h, plane, k)
+            for block, plane in jobs:
+                send(block, plane, k)
             return carry
 
         lax.fori_loop(1, 16, one, 0)
-        for h, plane in jobs:
+        for block, plane in jobs:
             if plane is z:
-                dst[h, me] = src[h, me]
+                src, dst, _, _ = block(me)
+                dst[...] = src[...]
             else:
-                send(src, dst, ssem, rsem, h, plane, 0)
+                send(block, plane, 0)
+
+    def tap_copy(step):
+        here = near_taps.at[core]
+        return pltpu.make_async_remote_copy(
+            src_ref=taps if step == 0 else here,
+            dst_ref=here,
+            send_sem=ss_t.at[step],
+            recv_sem=rs_t.at[step],
+            device_id=twin if step == 0 else {"dp": other_core},
+            device_id_type=MESH,
+        )
 
     first, second = order
     for n, plane in enumerate(planes):
@@ -143,30 +188,51 @@
         both[plane] = jnp.concatenate([kv, gg], axis=1)
         rows_of(first, plane)
         if n == 0:
-            pl.semaphore_wait(barrier, PARTS + 1)
-        if n < 2:
-            send_planes(send_a, recv_a, ss_a, rs_a, [(first, plane)])
+            taps[...] = flt[
+                :, pl.ds(pl.multiple_of(core * (LENGTH // 4), LENGTH // 4), LENGTH // 4)
+            ].astype(BF16)
+            pl.semaphore_wait(barrier, PARTS + 2)
+            tap_copy(0).start()
+            send_planes([(forward_block(first), plane)])
+    send_planes([(forward_block(first), p) for p in (beside, behind, z)])
     rows_of(second, across)
     rows_of(second, behind)
+    for n in range(2):
+        one_array = both[(1 - half) * 2 + n, :, pl.ds(pl.multiple_of(half * SPAN, SPAN), SPAN)]
+        work_a[pl.ds(n * 16, 16)] = dot_t(eye[...], one_array).astype(BF16).reshape(16, OWN, SPAN)
     send_planes(
-        send_a, recv_a, ss_a, rs_a,
-        [(first, beside), (second, across), (first, z), (second, behind)],
+        [
+            (forward_block(second), across), (work_block, beside),
+            (forward_block(second), behind), (work_block, z),
+        ]
     )
     rows_of(second, beside)
     rows_of(second, z)
-    send_planes(send_a, recv_a, ss_a, rs_a, [(second, beside), (second, z)])
-
-    def whole(src, dst, ssem, rsem, h):
+    send_planes([(forward_block(second), beside), (forward_block(second), z)])
+
+    def whole(src, dst, count, ssem, rsem):
         return pltpu.make_async_remote_copy(
-            src_ref=src.at[h, pl.ds(0, PARTS - 1)],
-            dst_ref=dst.at[h, pl.ds(0, PARTS - 1)],
-            send_sem=ssem.at[h],
-            recv_sem=rsem.at[h],
+            src_ref=src.at[pl.ds(0, count)],
+            dst_ref=dst.at[pl.ds(0, count)],
+            send_sem=ssem,
+            recv_sem=rsem,
             device_id={"context": me},
             device_id_type=MESH,
         )
 
-    for load in loads[5:]:
+    def forward_whole(h):
+        return whole(send_a.at[h], recv_a.at[h], PARTS - 1, ss_a.at[h], rs_a.at[h])
+
+    def return_whole(h):
+        return whole(send_b.at[h], recv_b.at[h], SIDE - 1, ss_b.at[h], rs_b.at[h])
+
+    def far_whole(h):
+        return whole(send_c.at[h], recv_c.at[h], SIDE, ss_c.at[h], rs_c.at[h])
+
+    work_whole = whole(work_a, work_in, SIDE - 1, ss_w.at[0], rs_w.at[0])
+    result_whole = whole(work_b, work_back, SIDE - 1, ss_w.at[1], rs_w.at[1])
+
+    for load in loads[7:]:
         load.wait()
 
     def lay(p, carry):
@@ -179,14 +245,15 @@
 
     lax.fori_loop(0, PARTS, lay, 0)
 
-    def column(ref, row):
+    def column(ref, row, parts=PARTS):
         return jnp.concatenate(
-            [ref[lanes, pl.ds(row, PARTS, stride=OWN), :] for lanes in range(2)], axis=1
+            [ref[lanes, pl.ds(row, parts, stride=OWN), :] for lanes in range(2)], axis=1
         )
 
-    def twist(mid):
-        re, im = mid[:PARTS], mid[PARTS:]
-        c, s = tcos[...], tsin[...]
+    def twist(mid, cos=tcos, sin=tsin):
+        parts = cos.shape[0]
+        re, im = mid[:parts], mid[parts:]
+        c, s = cos[...], sin[...]
         return jnp.concatenate([re * c + im * s, im * c - re * s], axis=1).astype(BF16)
 
     def filter_pair(i, carry):
@@ -201,6 +268,68 @@
         return carry
 
     lax.fori_loop(0, OWN // 2, filter_pair, 0)
+
+    def near_rows(i):
+        mids = []
+        for n in range(2):
+            x = [column(wide, 4 * i + 2 * n + m, SIDE) for m in range(2)]
+            mid = dot(near[...], jnp.concatenate(x, axis=0).astype(BF16))
+            for m in range(2):
+                mids.append(twist(mid[2 * m * SIDE : 2 * (m + 1) * SIDE], near_cos, near_sin))
+        return dot(jnp.concatenate(mids, axis=0), fwd[...])
+
+    tap_copy(0).wait_recv()
+    tap_copy(1).start()
+    tap_copy(1).wait_recv()
+    for q in range(2):
+        for p in range(SIDE // 2):
+            for lanes in range(2):
+                wide[lanes, pl.ds((q * SIDE // 2 + p) * OWN, OWN), :] = near_taps[
+                    q, :, pl.ds(p * SPAN + lanes * 128, 128)
+                ].astype(F32)
+
+    def near_filters(i, carry):
+        full = near_rows(i)
+        im = jnp.where(half == 0, full[:, SPAN:], -full[:, SPAN:])
+        full = jnp.concatenate([full[:, :SPAN], im], axis=1)
+        near_spec[pl.ds(4 * i, 4)] = full.reshape(4, SIDE, 2 * SPAN)
+        return carry
+
+    lax.fori_loop(0, OWN // 4, near_filters, 0)
+
+    def work():
+        for lanes in range(2):
+            wide[lanes, pl.ds(0, SIDE * OWN)] = (
+                work_in[:, :, pl.ds(lanes * 128, 128)].astype(F32).reshape(SIDE * OWN, 128)
+            )
+
+        def four(i, carry):
+            x = near_rows(i)
+            f = near_spec[pl.ds(4 * i, 4)].reshape(4 * SIDE, 2 * SPAN)
+            fr, fi = f[:, :SPAN], f[:, SPAN:]
+            xr, xi = x[:, :SPAN], x[:, SPAN:]
+            prod = jnp.concatenate([fr * xr - fi * xi, fr * xi + fi * xr], axis=1)
+            mid = dot(prod.astype(BF16), inv[...])
+            co, si = near_cos[...], near_sin[...]
+            for n in range(2):
+                parts = []
+                for m in range(2):
+                    top = (2 * n + m) * SIDE
+                    re, im = mid[top : top + SIDE, :SPAN], mid[top : top + SIDE, SPAN:]
+                    parts += [re * co - im * si, im * co + re * si]
+                line = dot(near_last[...], jnp.concatenate(parts, axis=0).astype(BF16))
+                for m in range(2):
+                    for lanes in range(2):
+                        back_wide[lanes, pl.ds(4 * i + 2 * n + m, SIDE, stride=OWN), :] = line[
+                            m * SIDE : (m + 1) * SIDE, lanes * 128 : (lanes + 1) * 128
+                        ]
+            return carry
+
+        lax.fori_loop(0, OWN // 4, four, 0)
+        for lanes in range(2):
+            work_b[:, :, pl.ds(lanes * 128, 128)] = (
+                back_wide[lanes, pl.ds(0, SIDE * OWN)].astype(BF16).reshape(SIDE, OWN, 128)
+            )
 
     def convolve(h, slot):
         for lanes in range(2):
@@ -247,10 +376,16 @@
             return carry
 
         lax.fori_loop(0, HALF // 2, channel_pair, 0)
+        here = pl.ds(pl.multiple_of(half * SIDE * OWN, OWN), SIDE * OWN)
+        there = pl.ds(pl.multiple_of((1 - half) * SIDE * OWN, OWN), SIDE * OWN)
+        chosen = []
         for lanes in range(2):
             send_b[h, :, :, pl.ds(lanes * 128, 128)] = (
-                back_wide[lanes].astype(BF16).reshape(PARTS, OWN, 128)
+                back_wide[lanes, here].astype(BF16).reshape(SIDE, OWN, 128)
             )
+            pieces = back_wide[lanes, there].reshape(SIDE, 2, HALF, 128)
+            chosen.append(jnp.where(half == 0, pieces[:, 0], pieces[:, 1]))
+        send_c[h] = jnp.concatenate(chosen, axis=1).astype(BF16)
 
     def lag_swap(slot):
         return pltpu.make_async_remote_copy(
@@ -272,16 +407,24 @@
     )
 
     for slot, h in enumerate(order):
-        whole(send_a, recv_a, ss_a, rs_a, h).wait_recv()
+        forward_whole(h).wait_recv()
         if slot == 1:
             lag_swap(0).wait_recv()
             far_out[...] = (lag[0, core] + lag_in[0].astype(F32)).astype(BF16)
             far.start()
         convolve(h, slot)
-        send_planes(send_b, recv_b, ss_b, rs_b, [(h, across), (h, behind)])
-        send_planes(send_b, recv_b, ss_b, rs_b, [(h, beside), (h, z)])
+        send_planes(
+            [
+                (far_block(h), across), (return_block(h), beside),
+                (far_block(h), behind), (return_block(h), z),
+            ]
+        )
         lag_out[slot] = lag[slot, 1 - core].astype(BF16)
         lag_swap(slot).start()
+        if slot == 0:
+            work_whole.wait_recv()
+            work()
+            send_planes([(work_result, beside), (work_result, z)])
 
     lag_swap(1).wait_recv()
     far.wait_recv()
@@ -291,20 +434,38 @@
             out_filter[:, pl.ds(p * SPAN + lanes * 128, 128)] = total[4 * p : 4 * p + 4]
 
     for h in order:
-        whole(send_b, recv_b, ss_b, rs_b, h).wait_recv()
-    for b in range(4):
-        cols = pl.ds(b * SPAN, SPAN)
-        groups = [recv_b[h, pl.ds(b * 16, 16)].astype(F32) for h in range(2)]
-        turned = []
-        for a in range(2):
-            rows = jnp.concatenate([g[:, a * HALF : (a + 1) * HALF] for g in groups], axis=1)
-            turned.append(dot_t(eye[...], rows.reshape(SPAN, SPAN).astype(BF16)))
-        out_conv[:, cols] = turned[0].astype(BF16)
-        out_back[:, cols] = turned[1].astype(BF16)
+        return_whole(h).wait_recv()
+        far_whole(h).wait_recv()
+    result_whole.wait_recv()
+
+    def turn(rows):
+        return dot_t(eye[...], rows.reshape(SPAN, SPAN).astype(BF16))
+
+    for n in range(2):
+        part = pl.ds(n * 16, 16)
+        cols = pl.ds(pl.multiple_of((half * 2 + n) * SPAN, SPAN), SPAN)
+        groups = [recv_b[h, part].astype(F32) for h in range(2)]
+        for a, out in enumerate((out_conv, out_back)):
+            rows = [g[:, a * HALF : (a + 1) * HALF] for g in groups]
+            out[:, cols] = turn(jnp.concatenate(rows, axis=1)).astype(BF16)
+        cols = pl.ds(pl.multiple_of(((1 - half) * 2 + n) * SPAN, SPAN), SPAN)
+        rows = []
+        for h in range(2):
+            pieces = recv_c[h, part].astype(F32)
+            rows.append(jnp.concatenate([pieces[:, :HALF], pieces[:, HALF:]], axis=2))
+        owner = turn(jnp.concatenate(rows, axis=1))
+        worker = turn(work_back[part])
+        out_conv[:, cols] = jnp.where(half == 0, worker, owner).astype(BF16)
+        out_back[:, cols] = jnp.where(half == 0, owner, worker).astype(BF16)
 
     for h in order:
-        whole(send_a, recv_a, ss_a, rs_a, h).wait_send()
-        whole(send_b, recv_b, ss_b, rs_b, h).wait_send()
+        forward_whole(h).wait_send()
+        return_whole(h).wait_send()
+        far_whole(h).wait_send()
+    work_whole.wait_send()
+    result_whole.wait_send()
+    for step in range(2):
+        tap_copy(step).wait_send()
     for slot in range(2):
         lag_swap(slot).wait_send()
     far.wait_send()
@@ -313,12 +474,13 @@
 def on_device(grad_out, gate, key_in, value_in, filters):
     vmem = pl.BlockSpec(memory_space=pltpu.VMEM)
     consts = [
-        jnp.asarray(t.astype(np.float32) if n in (2, 3) else np.asarray(t, dtype=jnp.bfloat16))
+        jnp.asarray(t.astype(np.float32) if n < 4 else np.asarray(t, dtype=jnp.bfloat16))
         for n, t in enumerate(tables())
     ]
-    place, *rest = consts
-    operands = (gate[0], key_in[0], value_in[0], grad_out[0], place, filters, *rest)
-    blocks = (2, PARTS, OWN, SPAN)
+    twists, (place, eye, *rest) = consts[:4], consts[4:]
+    operands = (
+        gate[0], key_in[0], value_in[0], grad_out[0], place, eye, filters, *twists, *rest,
+    )
     dma = pltpu.SemaphoreType.DMA
     seq = jax.ShapeDtypeStruct((SPAN, 1024), BF16)
     conv, back, grad_filter = pl.pallas_call(
@@ -330,20 +492,25 @@
             *[pltpu.VMEM(x.shape, x.dtype) for x in operands],
             dma((OPERANDS,)),
             pltpu.VMEM((4, SPAN, 2 * SPAN), BF16),
-            pltpu.VMEM(blocks, BF16),
-            pltpu.VMEM(blocks, BF16),
-            pltpu.VMEM(blocks, BF16),
-            pltpu.VMEM(blocks, BF16),
+            pltpu.VMEM((2, PARTS, OWN, SPAN), BF16),
+            pltpu.VMEM((2, PARTS, OWN, SPAN), BF16),
+            pltpu.VMEM((2, SIDE, OWN, SPAN), BF16),
+            pltpu.VMEM((2, SIDE, OWN, SPAN), BF16),
+            pltpu.VMEM((2, SIDE, OWN, 128), BF16),
+            pltpu.VMEM((2, SIDE, OWN, 128), BF16),
+            *[pltpu.VMEM((SIDE, OWN, SPAN), BF16)] * 4,
+            pltpu.VMEM((OWN, LENGTH // 4), BF16),
+            pltpu.VMEM((2, OWN, LENGTH // 4), BF16),
             pltpu.VMEM((2, PARTS * OWN, 128), F32),
             pltpu.VMEM((2, PARTS * OWN, 128), F32),
             pltpu.VMEM((OWN, PARTS, 2 * SPAN), F32),
+            pltpu.VMEM((OWN, SIDE, 2 * SPAN), F32),
             pltpu.VMEM((2, 2, 2, PARTS * 4, 128), F32),
             pltpu.VMEM((2, 2, PARTS * 4, 128), BF16),
             pltpu.VMEM((2, 2, PARTS * 4, 128), BF16),
             pltpu.VMEM((2, PARTS * 4, 128), BF16),
             pltpu.VMEM((2, PARTS * 4, 128), BF16),
-            dma((2,)), dma((2,)), dma((2,)), dma((2,)),
-            dma((2,)), dma((2,)), dma((1,)), dma((1,)),
+            *[dma((2,))] * 12, dma((1,)), dma((1,)),
         ],
         name="hyena_backward",
         compiler_params=pltpu.CompilerParams(

time: 71.1 us -> 63.3 us (0.89)
  Pallas kernels: 66.5 us -> 58.4 us
    pallas_call x1, Pallas kernels: 66.5 us -> 58.4 us  [on_device(): pl.pallas_call(kernel, out_shape=(seq, seq, jax.ShapeDtypeStruct((4, LENG...]
where the time goes in v2:
time: 63.3 us; the launch traced here: 62.8 us
  Pallas kernels  58.4 us (92%)
  other arithmetic  3.11 us (5%)
  local copies, waits for them, and re-layouts  0.71 us (1%)
  between operations  0.66 us (1%)
    pallas_call x1, Pallas kernels, on_device(): pl.pallas_call(kernel, out_shape=(seq, seq, jax.ShapeDtypeStruct((4, LENG...  58.4 us
    broadcast_in_dim x1, other arithmetic, on_device(): return (grad_gate[None], grad_key[None], grad_value[None], grad_filter)  3.11 us

profile of v2, /device:TPU:1, one launch (start us, length us, event | category | flops | bytes accessed | tf_op | source)
XLA Modules:
  0.0 62.8 jit_solution(7074930347947075161)
XLA Ops:
  0.6 0.0 copy-start
  0.6 58.4 %hyena_backward.1 = (bf16[256,1024]{1,0:T(8,128)(2,1)}, bf16[256,1024]{1,0:T(8,128)(2,1)}, f32[4,16384]{1,0:T(4,128)}) custom-call(bf16[256,1024]{1,0:T(8,128)(2,1)} %bitcast.16, bf16[256,1024]{1,0:T(8,128)(2,1)} %bitcast.13, bf16[256,1024]{1,0:T(8,128)(2,1)} %bitcast.14, bf16[256,1024]{1,0:T(8,128)(2,1)} %bitcast.15, ...), custom_call_target="tpu_custom_call" | custom-call | tf_op jit(solution)/shard_map/hyena_backward/pallas_call | solution.py:486
  59.0 0.0 copy-done
  59.0 0.0 copy-start.1
  59.0 3.1 %fusion.3 = (bf16[1,256,1024]{2,1,0:T(8,128)(2,1)}, bf16[1,256,1024]{2,1,0:T(8,128)(2,1)}, bf16[1,256,1024]{2,1,0:T(8,128)(2,1)}) fusion(bf16[256,1024]{1,0:T(8,128)(2,1)} %get-tuple-element.8, bf16[1,256,1024]{2,1,0:T(8,128)(2,1)S(1)} %copy-done, bf16[1,256,1024]{2,1,0:T(8,128)(2,1)} %param.21, bf16[256,1024]{1,0:T(8,128)(2,1)} %get-tuple-element.7, ...), kind=kLoop, calls=%fused_computation.6 | loop fusion | flops 2883584 | bytes 4194304 | tf_op jit(solution)/shard_map/broadcast_in_dim | solution.py:524
  62.1 0.0 copy-done.1
  62.1 0.7 %copy.23 = f32[4,16384]{1,0:T(4,128)} copy(f32[4,16384]{1,0:T(4,128)S(1)} %copy-done.1) | data formatting | bytes 524288
Async XLA Ops:
  0.6 58.4 %copy-start = (bf16[1,256,1024]{2,1,0:T(8,128)(2,1)S(1)}, bf16[1,256,1024]{2,1,0:T(8,128)(2,1)}, u32[]{:S(2)}) copy-start(bf16[1,256,1024]{2,1,0:T(8,128)(2,1)} %param.20) | copy-start | bytes 1572868
  59.0 3.1 %copy-start.1 = (f32[4,16384]{1,0:T(4,128)S(1)}, f32[4,16384]{1,0:T(4,128)}, u32[]{:S(2)}) copy-start(f32[4,16384]{1,0:T(4,128)} %get-tuple-element.20) | copy-start | bytes 786436

commit v3 on v2

--- a/solution.py
+++ b/solution.py
@@ -89,7 +89,7 @@
     out_conv, out_back, out_filter,
     both, send_a, recv_a, send_b, recv_b, send_c, recv_c, work_a, work_in, work_b, work_back,
     taps, near_taps, wide, back_wide, spec, near_spec, lag, lag_out, lag_in, far_out, far_in,
-    ss_a, rs_a, ss_b, rs_b, ss_c, rs_c, ss_w, rs_w, ss_t, rs_t, ss_l, rs_l, ss_f, rs_f,
+    ss_a, rs_a, ss_b, rs_b, ss_c, rs_c, ss_w, rs_w, ss_t, rs_t, ss_l, rs_l, ss_f, rs_f, cross,
 ):
     dp, me = lax.axis_index("dp"), lax.axis_index("context")
     z_hi, core = dp // 2, dp % 2
@@ -114,9 +114,8 @@
 
         lax.fori_loop(1 if plane is z else 0, 16, greet, 0)
     pl.semaphore_signal(barrier, inc=1, device_id={"dp": other_core}, device_id_type=MESH)
-    pl.semaphore_signal(barrier, inc=1, device_id={"dp": other_cube}, device_id_type=MESH)
     twin = {"dp": other_cube, "context": (me + SIDE) % PARTS}
-    pl.semaphore_signal(barrier, inc=1, device_id=twin, device_id_type=MESH)
+    partners = ({"dp": other_cube}, twin)
 
     for load in loads[:7]:
         load.wait()
@@ -191,10 +190,27 @@
             taps[...] = flt[
                 :, pl.ds(pl.multiple_of(core * (LENGTH // 4), LENGTH // 4), LENGTH // 4)
             ].astype(BF16)
-            pl.semaphore_wait(barrier, PARTS + 2)
-            tap_copy(0).start()
+            pl.semaphore_wait(barrier, PARTS + 2 * z_hi)
+
+            @pl.when(z_hi == 0)
+            def _():
+                for partner in partners:
+                    pl.semaphore_signal(barrier, inc=1, device_id=partner, device_id_type=MESH)
+
+            @pl.when(z_hi == 1)
+            def _():
+                for partner in partners:
+                    pl.semaphore_signal(cross, inc=1, device_id=partner, device_id_type=MESH)
+                tap_copy(0).start()
+
             send_planes([(forward_block(first), plane)])
     send_planes([(forward_block(first), p) for p in (beside, behind, z)])
+
+    @pl.when(z_hi == 0)
+    def _():
+        pl.semaphore_wait(cross, 2)
+        tap_copy(0).start()
+
     rows_of(second, across)
     rows_of(second, behind)
     for n in range(2):
@@ -278,16 +294,6 @@
                 mids.append(twist(mid[2 * m * SIDE : 2 * (m + 1) * SIDE], near_cos, near_sin))
         return dot(jnp.concatenate(mids, axis=0), fwd[...])
 
-    tap_copy(0).wait_recv()
-    tap_copy(1).start()
-    tap_copy(1).wait_recv()
-    for q in range(2):
-        for p in range(SIDE // 2):
-            for lanes in range(2):
-                wide[lanes, pl.ds((q * SIDE // 2 + p) * OWN, OWN), :] = near_taps[
-                    q, :, pl.ds(p * SPAN + lanes * 128, 128)
-                ].astype(F32)
-
     def near_filters(i, carry):
         full = near_rows(i)
         im = jnp.where(half == 0, full[:, SPAN:], -full[:, SPAN:])
@@ -295,7 +301,14 @@
         near_spec[pl.ds(4 * i, 4)] = full.reshape(4, SIDE, 2 * SPAN)
         return carry
 
-    lax.fori_loop(0, OWN // 4, near_filters, 0)
+    def near_spectrum():
+        for q in range(2):
+            for p in range(SIDE // 2):
+                for lanes in range(2):
+                    wide[lanes, pl.ds((q * SIDE // 2 + p) * OWN, OWN), :] = near_taps[
+                        q, :, pl.ds(p * SPAN + lanes * 128, 128)
+                    ].astype(F32)
+        lax.fori_loop(0, OWN // 4, near_filters, 0)
 
     def work():
         for lanes in range(2):
@@ -412,6 +425,9 @@
             lag_swap(0).wait_recv()
             far_out[...] = (lag[0, core] + lag_in[0].astype(F32)).astype(BF16)
             far.start()
+        else:
+            tap_copy(0).wait_recv()
+            tap_copy(1).start()
         convolve(h, slot)
         send_planes(
             [
@@ -422,6 +438,8 @@
         lag_out[slot] = lag[slot, 1 - core].astype(BF16)
         lag_swap(slot).start()
         if slot == 0:
+            tap_copy(1).wait_recv()
+            near_spectrum()
             work_whole.wait_recv()
             work()
             send_planes([(work_result, beside), (work_result, z)])
@@ -511,10 +529,11 @@
             pltpu.VMEM((2, PARTS * 4, 128), BF16),
             pltpu.VMEM((2, PARTS * 4, 128), BF16),
             *[dma((2,))] * 12, dma((1,)), dma((1,)),
+            pltpu.SemaphoreType.REGULAR,
         ],
         name="hyena_backward",
         compiler_params=pltpu.CompilerParams(
-            collective_id=0, has_side_effects=True, vmem_limit_bytes=63 * 2**20
+            collective_id=0, has_side_effects=True, vmem_limit_bytes=58 * 2**20
         ),
     )(*operands)
     wide = back.astype(F32)

time: 63.3 us -> 61.8 us (0.976)
  Pallas kernels: 58.4 us -> 57.5 us
    pallas_call x1, Pallas kernels: 58.4 us -> 57.5 us  [on_device(): pl.pallas_call(kernel, out_shape=(seq, seq, jax.ShapeDtypeStruct((4, LENG...]
where the time goes in v3:
time: 61.8 us; the launch traced here: 61.7 us
  Pallas kernels  57.5 us (93%)
  other arithmetic  2.79 us (5%)
  local copies, waits for them, and re-layouts  0.72 us (1%)
  between operations  0.7 us (1%)
    pallas_call x1, Pallas kernels, on_device(): pl.pallas_call(kernel, out_shape=(seq, seq, jax.ShapeDtypeStruct((4, LENG...  57.5 us
    broadcast_in_dim x1, other arithmetic, on_device(): return (grad_gate[None], grad_key[None], grad_value[None], grad_filter)  2.79 us

profile of v3, /device:TPU:1, one launch (start us, length us, event | category | flops | bytes accessed | tf_op | source)
XLA Modules:
  0.0 61.7 jit_solution(5224002361285864744)
XLA Ops:
  0.6 0.0 copy-start
  0.6 0.0 copy-start.1
  0.7 0.0 copy-start.2
  0.7 57.5 %hyena_backward.1 = (bf16[256,1024]{1,0:T(8,128)(2,1)}, bf16[256,1024]{1,0:T(8,128)(2,1)}, f32[4,16384]{1,0:T(4,128)}) custom-call(bf16[256,1024]{1,0:T(8,128)(2,1)} %bitcast.16, bf16[256,1024]{1,0:T(8,128)(2,1)} %bitcast.13, bf16[256,1024]{1,0:T(8,128)(2,1)} %bitcast.14, bf16[256,1024]{1,0:T(8,128)(2,1)} %bitcast.15, ...), custom_call_target="tpu_custom_call" | custom-call | tf_op jit(solution)/shard_map/hyena_backward/pallas_call | solution.py:504
  58.2 0.0 copy-done
  58.2 0.0 copy-done.1
  58.2 0.0 copy-done.2
  58.2 0.0 copy-start.3
  58.2 2.8 %fusion.3 = (bf16[1,256,1024]{2,1,0:T(8,128)(2,1)}, bf16[1,256,1024]{2,1,0:T(8,128)(2,1)}, bf16[1,256,1024]{2,1,0:T(8,128)(2,1)}) fusion(bf16[256,1024]{1,0:T(8,128)(2,1)} %get-tuple-element.8, bf16[1,256,1024]{2,1,0:T(8,128)(2,1)S(1)} %copy-done, bf16[1,256,1024]{2,1,0:T(8,128)(2,1)S(1)} %copy-done.1, bf16[256,1024]{1,0:T(8,128)(2,1)} %get-tuple-element.7, ...), kind=kLoop, calls=%fused_computation.6 | loop fusion | flops 2883584 | bytes 4194304 | tf_op jit(solution)/shard_map/broadcast_in_dim | solution.py:543
  61.0 0.0 copy-done.3
  61.0 0.7 %copy.23 = f32[4,16384]{1,0:T(4,128)} copy(f32[4,16384]{1,0:T(4,128)S(1)} %copy-done.3) | data formatting | bytes 524288
Async XLA Ops:
  0.6 57.5 %copy-start = (bf16[1,256,1024]{2,1,0:T(8,128)(2,1)S(1)}, bf16[1,256,1024]{2,1,0:T(8,128)(2,1)}, u32[]{:S(2)}) copy-start(bf16[1,256,1024]{2,1,0:T(8,128)(2,1)} %param.20) | copy-start | bytes 1572868
  0.6 57.5 %copy-start.1 = (bf16[1,256,1024]{2,1,0:T(8,128)(2,1)S(1)}, bf16[1,256,1024]{2,1,0:T(8,128)(2,1)}, u32[]{:S(2)}) copy-start(bf16[1,256,1024]{2,1,0:T(8,128)(2,1)} %param.21) | copy-start | bytes 1572868
  0.7 57.5 %copy-start.2 = (bf16[1,256,1024]{2,1,0:T(8,128)(2,1)S(1)}, bf16[1,256,1024]{2,1,0:T(8,128)(2,1)}, u32[]{:S(2)}) copy-start(bf16[1,256,1024]{2,1,0:T(8,128)(2,1)} %param.18) | copy-start | bytes 1572868
  58.2 2.8 %copy-start.3 = (f32[4,16384]{1,0:T(4,128)S(1)}, f32[4,16384]{1,0:T(4,128)}, u32[]{:S(2)}) copy-start(f32[4,16384]{1,0:T(4,128)} %get-tuple-element.20) | copy-start | bytes 786436

commit v4 on v3

--- a/solution.py
+++ b/solution.py
@@ -71,7 +71,7 @@
 
 def kernel(*refs):
     given, refs = refs[:OPERANDS], refs[OPERANDS:]
-    results, refs = refs[:3], refs[3:]
+    results, refs = refs[:4], refs[4:]
     held, loaded, refs = refs[:OPERANDS], refs[OPERANDS], refs[OPERANDS + 1 :]
     loads = [
         pltpu.make_async_copy(src, dst, loaded.at[n])
@@ -86,10 +86,10 @@
     loads,
     gt, ki, vi, go, place, eye, flt, tcos, tsin, near_cos, near_sin,
     filt, fwd, near, pair, inv, last, near_last,
-    out_conv, out_back, out_filter,
-    both, send_a, recv_a, send_b, recv_b, send_c, recv_c, work_a, work_in, work_b, work_back,
-    taps, near_taps, wide, back_wide, spec, near_spec, lag, lag_out, lag_in, far_out, far_in,
-    ss_a, rs_a, ss_b, rs_b, ss_c, rs_c, ss_w, rs_w, ss_t, rs_t, ss_l, rs_l, ss_f, rs_f, cross,
+    recv_b, recv_c, work_back, out_filter,
+    both, send_a, recv_a, send_b, send_c, work_a, work_in, work_b,
+    taps, near_taps, wide, back_wide, spec, near_spec, lag, lag_out, lag_in, far_out, far_in, lag_sum,
+    ss_a, rs_a, ss_b, rs_b, ss_c, rs_c, ss_w, rs_w, ss_t, rs_t, ss_l, rs_l, ss_f, rs_f, kept, cross,
 ):
     dp, me = lax.axis_index("dp"), lax.axis_index("context")
     z_hi, core = dp // 2, dp % 2
@@ -128,23 +128,25 @@
     mine = me % SIDE
 
     def forward_block(h):
-        return lambda d: (send_a.at[h, d], recv_a.at[h, me], ss_a.at[h], rs_a.at[h])
+        return lambda d: (send_a.at[h, d], recv_a.at[h, me], ss_a.at[h], rs_a.at[h], None)
 
     def work_block(d):
-        return work_a.at[d % SIDE], work_in.at[mine], ss_w.at[0], rs_w.at[0]
+        return work_a.at[d % SIDE], work_in.at[mine], ss_w.at[0], rs_w.at[0], None
 
     def return_block(h):
-        return lambda d: (send_b.at[h, d % SIDE], recv_b.at[h, mine], ss_b.at[h], rs_b.at[h])
+        return lambda d: (
+            send_b.at[h, d % SIDE], recv_b.at[h, mine], ss_b.at[h], rs_b.at[h], kept.at[h],
+        )
 
     def far_block(h):
-        return lambda d: (send_c.at[h, d % SIDE], recv_c.at[h, mine], ss_c.at[h], rs_c.at[h])
+        return lambda d: (send_c.at[h, d % SIDE], recv_c.at[h, mine], ss_c.at[h], rs_c.at[h], None)
 
     def work_result(d):
-        return work_b.at[d % SIDE], work_back.at[mine], ss_w.at[1], rs_w.at[1]
+        return work_b.at[d % SIDE], work_back.at[mine], ss_w.at[1], rs_w.at[1], kept.at[2]
 
     def send(block, plane, k):
         d = target(me, plane, k)
-        src, dst, ssem, rsem = block(d)
+        src, dst, ssem, rsem, _ = block(d)
         pltpu.make_async_remote_copy(
             src_ref=src,
             dst_ref=dst,
@@ -163,8 +165,11 @@
         lax.fori_loop(1, 16, one, 0)
         for block, plane in jobs:
             if plane is z:
-                src, dst, _, _ = block(me)
-                dst[...] = src[...]
+                src, dst, _, _, own = block(me)
+                if own is None:
+                    dst[...] = src[...]
+                else:
+                    pltpu.make_async_copy(src, dst, own).start()
             else:
                 send(block, plane, 0)
 
@@ -449,32 +454,18 @@
     for lanes in range(2):
         total = lag[1, core, lanes] + lag_in[1, lanes].astype(F32) + far_in[lanes].astype(F32)
         for p in range(PARTS):
-            out_filter[:, pl.ds(p * SPAN + lanes * 128, 128)] = total[4 * p : 4 * p + 4]
+            lag_sum[:, pl.ds(p * SPAN + lanes * 128, 128)] = total[4 * p : 4 * p + 4]
+    lag_store = pltpu.make_async_copy(lag_sum, out_filter, kept.at[3])
+    lag_store.start()
 
     for h in order:
         return_whole(h).wait_recv()
         far_whole(h).wait_recv()
     result_whole.wait_recv()
 
-    def turn(rows):
-        return dot_t(eye[...], rows.reshape(SPAN, SPAN).astype(BF16))
-
-    for n in range(2):
-        part = pl.ds(n * 16, 16)
-        cols = pl.ds(pl.multiple_of((half * 2 + n) * SPAN, SPAN), SPAN)
-        groups = [recv_b[h, part].astype(F32) for h in range(2)]
-        for a, out in enumerate((out_conv, out_back)):
-            rows = [g[:, a * HALF : (a + 1) * HALF] for g in groups]
-            out[:, cols] = turn(jnp.concatenate(rows, axis=1)).astype(BF16)
-        cols = pl.ds(pl.multiple_of(((1 - half) * 2 + n) * SPAN, SPAN), SPAN)
-        rows = []
-        for h in range(2):
-            pieces = recv_c[h, part].astype(F32)
-            rows.append(jnp.concatenate([pieces[:, :HALF], pieces[:, HALF:]], axis=2))
-        owner = turn(jnp.concatenate(rows, axis=1))
-        worker = turn(work_back[part])
-        out_conv[:, cols] = jnp.where(half == 0, worker, owner).astype(BF16)
-        out_back[:, cols] = jnp.where(half == 0, owner, worker).astype(BF16)
+    for block in (return_block(0), return_block(1), work_result):
+        src, dst, _, _, own = block(me)
+        pltpu.make_async_copy(src, dst, own).wait()
 
     for h in order:
         forward_whole(h).wait_send()
@@ -487,10 +478,73 @@
     for slot in range(2):
         lag_swap(slot).wait_send()
     far.wait_send()
+    lag_store.wait()
+
+
+def finish(*refs):
+    given, results, held, made = refs[:7], refs[7:11], refs[11:18], refs[18:21]
+    loaded, stored = refs[21:]
+    near, far, work, go, vi, ki, lags = held
+    half = lax.axis_index("context") // SIDE
+
+    def columns(side, n):
+        plane = (half if side == 0 else 1 - half) * 2 + n
+        return pl.ds(pl.multiple_of(plane * SPAN, SPAN), SPAN)
+
+    def load(n, sem, view):
+        return pltpu.make_async_copy(view(given[n]), view(held[n]), loaded.at[sem])
+
+    steps, loads, sem = [(side, n) for side in range(2) for n in range(2)], [], 0
+    for side, n in steps:
+        part, cols = pl.ds(n * 16, 16), columns(side, n)
+        block = lambda ref: ref.at[:, part]
+        views = [(0, block)] if side == 0 else [(1, block), (2, lambda ref: ref.at[part])]
+        views += [(m, lambda ref: ref.at[:, cols]) for m in (3, 4, 5)]
+        group = []
+        for m, view in views:
+            group.append(load(m, sem, view))
+            group[-1].start()
+            sem += 1
+        loads.append(group)
+    passing = load(6, sem, lambda ref: ref)
+    passing.start()
+
+    def turn(rows):
+        return rows.reshape(SPAN, SPAN).astype(F32).T
+
+    stores = []
+    for step, (side, n) in enumerate(steps):
+        for one in loads[step]:
+            one.wait()
+        part, cols = pl.ds(n * 16, 16), columns(side, n)
+        if side == 0:
+            groups = [near[h, part].astype(F32) for h in range(2)]
+            conv, back = [
+                turn(jnp.concatenate([g[:, a * HALF : (a + 1) * HALF] for g in groups], axis=1))
+                for a in range(2)
+            ]
+        else:
+            pieces = [far[h, part].astype(F32) for h in range(2)]
+            pieces = [jnp.concatenate([q[:, :HALF], q[:, HALF:]], axis=2) for q in pieces]
+            owner, worker = turn(jnp.concatenate(pieces, axis=1)), turn(work[part])
+            conv, back = jnp.where(half == 0, worker, owner), jnp.where(half == 0, owner, worker)
+        for m, (left, right) in enumerate(((go, conv), (vi, back), (ki, back))):
+            made[m][:, cols] = (left[:, cols].astype(F32) * right).astype(BF16)
+            stores.append(
+                pltpu.make_async_copy(
+                    made[m].at[:, cols], results[m].at[:, cols], stored.at[3 * step + m]
+                )
+            )
+            stores[-1].start()
+        if step == 1:
+            passing.wait()
+            stores.append(pltpu.make_async_copy(lags, results[3], stored.at[12]))
+            stores[-1].start()
+    for one in stores:
+        one.wait()
 
 
 def on_device(grad_out, gate, key_in, value_in, filters):
-    vmem = pl.BlockSpec(memory_space=pltpu.VMEM)
     consts = [
         jnp.asarray(t.astype(np.float32) if n < 4 else np.asarray(t, dtype=jnp.bfloat16))
         for n, t in enumerate(tables())
@@ -501,11 +555,18 @@
     )
     dma = pltpu.SemaphoreType.DMA
     seq = jax.ShapeDtypeStruct((SPAN, 1024), BF16)
-    conv, back, grad_filter = pl.pallas_call(
+    lags = jax.ShapeDtypeStruct((4, LENGTH), F32)
+    hbm = pl.BlockSpec(memory_space=pltpu.HBM)
+    *blocks, grad_filter = pl.pallas_call(
         kernel,
-        out_shape=(seq, seq, jax.ShapeDtypeStruct((4, LENGTH), F32)),
-        in_specs=[pl.BlockSpec(memory_space=pltpu.HBM)] * OPERANDS,
-        out_specs=(vmem,) * 3,
+        out_shape=(
+            jax.ShapeDtypeStruct((2, SIDE, OWN, SPAN), BF16),
+            jax.ShapeDtypeStruct((2, SIDE, OWN, 128), BF16),
+            jax.ShapeDtypeStruct((SIDE, OWN, SPAN), BF16),
+            lags,
+        ),
+        in_specs=[hbm] * OPERANDS,
+        out_specs=(hbm,) * 4,
         scratch_shapes=[
             *[pltpu.VMEM(x.shape, x.dtype) for x in operands],
             dma((OPERANDS,)),
@@ -513,10 +574,8 @@
             pltpu.VMEM((2, PARTS, OWN, SPAN), BF16),
             pltpu.VMEM((2, PARTS, OWN, SPAN), BF16),
             pltpu.VMEM((2, SIDE, OWN, SPAN), BF16),
-            pltpu.VMEM((2, SIDE, OWN, SPAN), BF16),
             pltpu.VMEM((2, SIDE, OWN, 128), BF16),
-            pltpu.VMEM((2, SIDE, OWN, 128), BF16),
-            *[pltpu.VMEM((SIDE, OWN, SPAN), BF16)] * 4,
+            *[pltpu.VMEM((SIDE, OWN, SPAN), BF16)] * 3,
             pltpu.VMEM((OWN, LENGTH // 4), BF16),
             pltpu.VMEM((2, OWN, LENGTH // 4), BF16),
             pltpu.VMEM((2, PARTS * OWN, 128), F32),
@@ -528,7 +587,8 @@
             pltpu.VMEM((2, 2, PARTS * 4, 128), BF16),
             pltpu.VMEM((2, PARTS * 4, 128), BF16),
             pltpu.VMEM((2, PARTS * 4, 128), BF16),
-            *[dma((2,))] * 12, dma((1,)), dma((1,)),
+            pltpu.VMEM((4, LENGTH), F32),
+            *[dma((2,))] * 12, dma((1,)), dma((1,)), dma((4,)),
             pltpu.SemaphoreType.REGULAR,
         ],
         name="hyena_backward",
@@ -536,11 +596,22 @@
             collective_id=0, has_side_effects=True, vmem_limit_bytes=58 * 2**20
         ),
     )(*operands)
-    wide = back.astype(F32)
-    grad_gate = (grad_out[0].astype(F32) * conv.astype(F32)).astype(BF16)
-    grad_key = (wide * value_in[0].astype(F32)).astype(BF16)
-    grad_value = (wide * key_in[0].astype(F32)).astype(BF16)
-    return (grad_gate[None], grad_key[None], grad_value[None], grad_filter)
+    operands = (*blocks, grad_out[0], value_in[0], key_in[0], grad_filter)
+    grads = pl.pallas_call(
+        finish,
+        out_shape=(seq, seq, seq, lags),
+        in_specs=[hbm] * 7,
+        out_specs=(hbm,) * 4,
+        scratch_shapes=[
+            *[pltpu.VMEM(x.shape, x.dtype) for x in operands],
+            *[pltpu.VMEM(seq.shape, seq.dtype)] * 3,
+            dma((21,)),
+            dma((13,)),
+        ],
+        name="products",
+        compiler_params=pltpu.CompilerParams(vmem_limit_bytes=60 * 2**20),
+    )(*operands)
+    return (grads[0][None], grads[1][None], grads[2][None], grads[3])
 
 
 def solution(mesh):

time: 61.8 us -> 60.1 us (0.972)
  other arithmetic: 2.79 us -> 0 us
  Pallas kernels: 57.5 us -> 59.4 us
  local copies, waits for them, and re-layouts: 0.72 us -> 0 us
    broadcast_in_dim x1 -> x0, other arithmetic: 2.79 us -> none  [on_device(): return (grad_gate[None], grad_key[None], grad_value[None], grad_filter)]
    pallas_call x1 -> x2, Pallas kernels: 57.5 us -> 59.4 us  [the longest x1 56.1 us: on_device(): pl.pallas_call(kernel, out_shape=(jax.ShapeDtypeStruct((2, SIDE, OWN, SPA...]
    unnamed x9 -> x0, local copies, waits for them, and re-layouts: 0.72 us -> none
where the time goes in v4:
time: 60.1 us; the launch traced here: 60 us
  Pallas kernels  59.4 us (99%)
  between operations  0.64 us (1%)
    pallas_call x1, Pallas kernels, on_device(): pl.pallas_call(kernel, out_shape=(jax.ShapeDtypeStruct((2, SIDE, OWN, SPA...  56.1 us
    pallas_call x1, Pallas kernels, on_device(): pl.pallas_call(finish, out_shape=(seq, seq, seq, lags), in_specs=[hbm] *...  3.26 us

profile of v4, /device:TPU:1, one launch (start us, length us, event | category | flops | bytes accessed | tf_op | source)
XLA Modules:
  0.0 60.0 jit_solution(11134771645625569950)
XLA Ops:
  0.6 56.1 %hyena_backward.1 = (bf16[2,32,16,256]{3,2,1,0:T(8,128)(2,1)}, bf16[2,32,16,128]{3,2,1,0:T(8,128)(2,1)}, bf16[32,16,256]{2,1,0:T(8,128)(2,1)}, f32[4,16384]{1,0:T(4,128)}) custom-call(bf16[256,1024]{1,0:T(8,128)(2,1)} %bitcast.13, bf16[256,1024]{1,0:T(8,128)(2,1)} %bitcast.7, bf16[256,1024]{1,0:T(8,128)(2,1)} %bitcast.9, bf16[256,1024]{1,0:T(8,128)(2,1)} %bitcast.11, ...), custom_call_target="tpu_custom_call" | custom-call | tf_op jit(solution)/shard_map/hyena_backward/pallas_call | solution.py:560
  56.7 3.3 %products.1 = (bf16[256,1024]{1,0:T(8,128)(2,1)}, bf16[256,1024]{1,0:T(8,128)(2,1)}, bf16[256,1024]{1,0:T(8,128)(2,1)}, f32[4,16384]{1,0:T(4,128)}) custom-call(bf16[2,32,16,256]{3,2,1,0:T(8,128)(2,1)} %get-tuple-element.12.refs_0_, bf16[2,32,16,128]{3,2,1,0:T(8,128)(2,1)} %get-tuple-element.13.refs_1_, bf16[32,16,256]{2,1,0:T(8,128)(2,1)} %get-tuple-element.14.refs_2_, ...), custom_call_target="tpu_custom_call" | custom-call | tf_op jit(solution)/shard_map/products/pallas_call | solution.py:600

commit v5 on v4

--- a/solution.py
+++ b/solution.py
@@ -126,6 +126,7 @@
         send_a[h, pl.ds(plane * 16, 16)] = rows.reshape(16, OWN, SPAN)
 
     mine = me % SIDE
+    sums = pl.ds(0, PARTS * 4)
 
     def forward_block(h):
         return lambda d: (send_a.at[h, d], recv_a.at[h, me], ss_a.at[h], rs_a.at[h], None)
@@ -351,7 +352,7 @@
 
     def convolve(h, slot):
         for lanes in range(2):
-            wide[lanes] = (
+            wide[lanes, pl.ds(0, PARTS * OWN)] = (
                 recv_a[h, :, :, pl.ds(lanes * 128, 128)].astype(F32).reshape(PARTS * OWN, 128)
             )
 
@@ -428,7 +429,7 @@
         forward_whole(h).wait_recv()
         if slot == 1:
             lag_swap(0).wait_recv()
-            far_out[...] = (lag[0, core] + lag_in[0].astype(F32)).astype(BF16)
+            far_out[...] = (lag[0, core, :, sums] + lag_in[0].astype(F32)).astype(BF16)
             far.start()
         else:
             tap_copy(0).wait_recv()
@@ -440,7 +441,7 @@
                 (far_block(h), behind), (return_block(h), z),
             ]
         )
-        lag_out[slot] = lag[slot, 1 - core].astype(BF16)
+        lag_out[slot] = lag[slot, 1 - core, :, sums].astype(BF16)
         lag_swap(slot).start()
         if slot == 0:
             tap_copy(1).wait_recv()
@@ -452,7 +453,7 @@
     lag_swap(1).wait_recv()
     far.wait_recv()
     for lanes in range(2):
-        total = lag[1, core, lanes] + lag_in[1, lanes].astype(F32) + far_in[lanes].astype(F32)
+        total = lag[1, core, lanes, sums] + lag_in[1, lanes].astype(F32) + far_in[lanes].astype(F32)
         for p in range(PARTS):
             lag_sum[:, pl.ds(p * SPAN + lanes * 128, 128)] = total[4 * p : 4 * p + 4]
     lag_store = pltpu.make_async_copy(lag_sum, out_filter, kept.at[3])
@@ -578,11 +579,11 @@
             *[pltpu.VMEM((SIDE, OWN, SPAN), BF16)] * 3,
             pltpu.VMEM((OWN, LENGTH // 4), BF16),
             pltpu.VMEM((2, OWN, LENGTH // 4), BF16),
-            pltpu.VMEM((2, PARTS * OWN, 128), F32),
-            pltpu.VMEM((2, PARTS * OWN, 128), F32),
+            pltpu.VMEM((2, (PARTS + 1) * OWN, 128), F32),
+            pltpu.VMEM((2, (PARTS + 1) * OWN, 128), F32),
             pltpu.VMEM((OWN, PARTS, 2 * SPAN), F32),
             pltpu.VMEM((OWN, SIDE, 2 * SPAN), F32),
-            pltpu.VMEM((2, 2, 2, PARTS * 4, 128), F32),
+            pltpu.VMEM((2, 2, 2, PARTS * 4 + 8, 128), F32),
             pltpu.VMEM((2, 2, PARTS * 4, 128), BF16),
             pltpu.VMEM((2, 2, PARTS * 4, 128), BF16),
             pltpu.VMEM((2, PARTS * 4, 128), BF16),

time: 60.1 us -> 60.1 us (level)
  no operation moved by 1% of the time
where the time goes in v5:
time: 60.1 us; the launch traced here: 60 us
  Pallas kernels  59.4 us (99%)
  between operations  0.64 us (1%)
    pallas_call x1, Pallas kernels, on_device(): pl.pallas_call(kernel, out_shape=(jax.ShapeDtypeStruct((2, SIDE, OWN, SPA...  56.1 us
    pallas_call x1, Pallas kernels, on_device(): pl.pallas_call(finish, out_shape=(seq, seq, seq, lags), in_specs=[hbm] *...  3.26 us

profile of v5, /device:TPU:1, one launch (start us, length us, event | category | flops | bytes accessed | tf_op | source)
XLA Modules:
  0.0 60.0 jit_solution(10920121503109587793)
XLA Ops:
  0.6 56.1 %hyena_backward.1 = (bf16[2,32,16,256]{3,2,1,0:T(8,128)(2,1)}, bf16[2,32,16,128]{3,2,1,0:T(8,128)(2,1)}, bf16[32,16,256]{2,1,0:T(8,128)(2,1)}, f32[4,16384]{1,0:T(4,128)}) custom-call(bf16[256,1024]{1,0:T(8,128)(2,1)} %bitcast.13, bf16[256,1024]{1,0:T(8,128)(2,1)} %bitcast.7, bf16[256,1024]{1,0:T(8,128)(2,1)} %bitcast.9, bf16[256,1024]{1,0:T(8,128)(2,1)} %bitcast.11, ...), custom_call_target="tpu_custom_call" | custom-call | tf_op jit(solution)/shard_map/hyena_backward/pallas_call | solution.py:561
  56.7 3.3 %products.1 = (bf16[256,1024]{1,0:T(8,128)(2,1)}, bf16[256,1024]{1,0:T(8,128)(2,1)}, bf16[256,1024]{1,0:T(8,128)(2,1)}, f32[4,16384]{1,0:T(4,128)}) custom-call(bf16[2,32,16,256]{3,2,1,0:T(8,128)(2,1)} %get-tuple-element.12.refs_0_, bf16[2,32,16,128]{3,2,1,0:T(8,128)(2,1)} %get-tuple-element.13.refs_1_, bf16[32,16,256]{2,1,0:T(8,128)(2,1)} %get-tuple-element.14.refs_2_, ...), custom_call_target="tpu_custom_call" | custom-call | tf_op jit(solution)/shard_map/products/pallas_call | solution.py:601
